TPU v7x, 32 devices: a whole 2x2x4 slice. The times are simulated.
32 devices in a mesh: groups: 2 (over x), item: 8 (over z, y), user: 2 (over core).
Axes of the slice: x: 2, y: 2, z: 4, core: 2. Of those that a mesh axis runs over, the one named last changes fastest.
Arguments:
- interactions: bfloat16 [4096, 8192], P(('groups', 'user'), 'item'), parts along dimension 0, may hold values from 0 to 2, as said below
- counts: int32 [16384], P('groups'), parts along dimension 0, may hold values from 512 to 2048
Outputs:
- similarity: float32 [16384, 8192], P(('groups', 'item', 'user')), parts along dimension 0
There are 2 independent parts, one for each index of `groups`. A program takes and returns all parts, laid end to end along the dimension named above; each array names one. Nothing has to cross between parts.
Inputs may be any that keep to these rules, and one draw needn't show every extreme that they name: `interactions`: about half of the entries are zero; the others lie between 0.25 and 2.
All inputs are finite; a program needn't handle non-finite values.
Results may differ from a plain program's by a relative error of at most 0.0003.
Values may be sent and summed in bfloat16 or wider, within the bound.
A program may use at most 128 MiB of HBM per device.

v0:
```python
import jax
import jax.numpy as jnp
from jax import lax
from jax.sharding import PartitionSpec as P


def from_behind(value, axis, steps):
    count = lax.axis_size(axis)
    pairs = [(source, (source + steps) % count) for source in range(count)]
    return lax.ppermute(value, axis, pairs)


def shards(interactions, counts):
    block_items = interactions.shape[1]
    item_count = lax.axis_size("item")
    user_count = lax.axis_size("user")
    my_block = lax.axis_index("item")
    my_user = lax.axis_index("user")
    half_rows = block_items // user_count
    count_float = counts.astype(jnp.float32)
    row_damp = lax.dynamic_slice_in_dim(
        count_float, my_block * block_items + my_user * half_rows, half_rows
    ) ** (-0.4)
    col_damp_all = count_float ** (-0.6)
    contract = (((0,), (0,)), ((), ()))

    def tile_of(panel_data):
        full_tile = lax.dot_general(
            interactions, panel_data, contract, preferred_element_type=jnp.float32
        )
        return lax.psum_scatter(full_tile, "user", scatter_dimension=0, tiled=True)

    def place_tile(result, panel_data, source):
        source = source % item_count
        col_damp = lax.dynamic_slice_in_dim(col_damp_all, source * block_items, block_items)
        scaled = tile_of(panel_data) * row_damp[:, None] * col_damp[None, :]
        return lax.dynamic_update_slice_in_dim(result, scaled, source * block_items, 1)

    def move_ahead(panel_data):
        return from_behind(panel_data, "item", 1)

    result = jnp.zeros((half_rows, block_items * item_count), jnp.float32)
    result = place_tile(result, interactions, my_block)

    def move_behind(panel_data):
        return from_behind(panel_data, "item", -1)

    forward_steps = item_count // 2
    backward_steps = item_count - 1 - forward_steps

    def two_turns(turn_index, carry_state):
        result, front_panel, back_panel = carry_state
        front_panel = move_ahead(front_panel)
        back_panel = move_behind(back_panel)
        result = place_tile(result, front_panel, my_block - turn_index - 1)
        result = place_tile(result, back_panel, my_block + turn_index + 1)
        return (result, front_panel, back_panel)

    result, front_panel, back_panel = lax.fori_loop(
        0, backward_steps, two_turns, (result, interactions, interactions)
    )
    front_panel = move_ahead(front_panel)
    result = place_tile(result, front_panel, my_block - forward_steps)
    return result


def solution(mesh):
    placed = (P(("groups", "user"), "item"), P("groups"))
    return jax.shard_map(
        shards,
        mesh=mesh,
        in_specs=placed,
        out_specs=P(("groups", "item", "user"), None),
        check_vma=False,
    )
```

profile of v0, /device:TPU:1, one launch (start us, length us, event | category | flops | bytes accessed | tf_op | source)
XLA Modules:
  0.0 496.0 jit_solution(8666283960224810786)
XLA Ops:
  6.5 6.6 %fusion.4 = f32[1024,1024]{1,0:T(8,128)} fusion(bf16[1024,1024]{1,0:T(8,128)(2,1)} %param.4), kind=kOutput, calls=%fused_computation.11 | convolution fusion | flops 2147483648 | bytes 6291456 | tf_op jit(solution)/shard_map/dot_general | solution.py:28
  13.2 1.5 copy-done.3
  17.5 10.4 %reduce-scatter.5.cloned.1.call-done = f32[512,1024]{1,0:T(8,128)} async-done(((f32[1024,1024]{1,0:T(8,128)}), f32[512,1024]{1,0:T(8,128)}) %reduce-scatter.5.cloned.1.call-update) | async-done | bytes 2097168 | tf_op jit(solution)/shard_map/reduce_scatter | solution.py:31
  28.0 2.0 broadcast_in_dim.12
  30.2 6.2 %copy-done.2 = f32[512,8192]{1,0:T(8,128)} copy-done((f32[512,8192]{1,0:T(8,128)}, f32[512,8192]{1,0:T(8,128)S(1)}, u32[]{:S(2)}) %copy-start.2) | copy-done | bytes 16777240
  36.4 383.8 %while.19 = (s32[]{:T(128)}, f32[512,8192]{1,0:T(8,128)}, bf16[1024,1024]{1,0:T(8,128)(2,1)}, bf16[1024,1024]{1,0:T(8,128)(2,1)}, bf16[1024,1024]{1,0:T(8,128)(2...) while((s32[]{:T(128)}, f32[512,8192]{1,0:T(8,128)}, ...), condition=%wide.region_4.5_spmd, body=%wide.region_1.4_spmd.sunk | while | flops 4297064448 | bytes 113275648 | solution.py:59
  37.8 48.7 %collective-permute-done = bf16[1024,1024]{1,0:T(8,128)(2,1)S(1)} collective-permute-done((bf16[1024,1024]{1,0:T(8,128)(2,1)}, bf16[1024,1024]{1,0:T(8,128)(2,1)S(1)}, u32[]{:S(2)}, u32[]{:S(2)}) %collective-permute-start) | collective-permute-done | bytes 2097184 | tf_op jit(solution)/shard_map/while/body/eval_jaxpr/ppermute | solution.py:10
  86.5 5.9 %fusion.24 = f32[1024,1024]{1,0:T(8,128)} fusion(bf16[1024,1024]{1,0:T(8,128)(2,1)} %get-tuple-element.353, bf16[1024,1024]{1,0:T(8,128)(2,1)S(1)} %collective-permute-done), kind=kOutput, calls=%fused_computation.9.clone.1 | convolution fusion | flops 2147483648 | bytes 8388608 | tf_op jit(solution)/shard_map/while/body/eval_jaxpr/dot_general | solution.py:28
  93.8 45.2 %collective-permute-done.1 = bf16[1024,1024]{1,0:T(8,128)(2,1)S(1)} collective-permute-done((bf16[1024,1024]{1,0:T(8,128)(2,1)}, bf16[1024,1024]{1,0:T(8,128)(2,1)S(1)}, u32[]{:S(2)}, u32[]{:S(2)}) %collective-permute-start.1) | collective-permute-done | bytes 2097184 | tf_op jit(solution)/shard_map/while/body/eval_jaxpr/ppermute | solution.py:10
  140.3 6.0 %fusion.26 = f32[1024,1024]{1,0:T(8,128)} fusion(bf16[1024,1024]{1,0:T(8,128)(2,1)} %get-tuple-element.353, bf16[1024,1024]{1,0:T(8,128)(2,1)S(1)} %collective-permute-done.1), kind=kOutput, calls=%fused_computation.10.clone.1 | convolution fusion | flops 2147483648 | bytes 8388608 | tf_op jit(solution)/shard_map/while/body/eval_jaxpr/dot_general | solution.py:28
  150.0 3.1 multiply_dynamic-update-slice_fusion.6
  153.2 7.9 %reduce-scatter.11.cloned.1.call-done = f32[512,1024]{1,0:T(8,128)} async-done(((f32[1024,1024]{1,0:T(8,128)}), f32[512,1024]{1,0:T(8,128)}) %reduce-scatter.11.cloned.1.call-update) | async-done | bytes 2097168 | tf_op jit(solution)/shard_map/while/body/eval_jaxpr/reduce_scatter | solution.py:31
  161.0 3.3 multiply_dynamic-update-slice_fusion.7
  165.8 48.6 %collective-permute-done = bf16[1024,1024]{1,0:T(8,128)(2,1)S(1)} collective-permute-done((bf16[1024,1024]{1,0:T(8,128)(2,1)}, bf16[1024,1024]{1,0:T(8,128)(2,1)S(1)}, u32[]{:S(2)}, u32[]{:S(2)}) %collective-permute-start) | collective-permute-done | bytes 2097184 | tf_op jit(solution)/shard_map/while/body/eval_jaxpr/ppermute | solution.py:10
  214.4 5.9 %fusion.24 = f32[1024,1024]{1,0:T(8,128)} fusion(bf16[1024,1024]{1,0:T(8,128)(2,1)} %get-tuple-element.353, bf16[1024,1024]{1,0:T(8,128)(2,1)S(1)} %collective-permute-done), kind=kOutput, calls=%fused_computation.9.clone.1 | convolution fusion | flops 2147483648 | bytes 8388608 | tf_op jit(solution)/shard_map/while/body/eval_jaxpr/dot_general | solution.py:28
  221.7 45.1 %collective-permute-done.1 = bf16[1024,1024]{1,0:T(8,128)(2,1)S(1)} collective-permute-done((bf16[1024,1024]{1,0:T(8,128)(2,1)}, bf16[1024,1024]{1,0:T(8,128)(2,1)S(1)}, u32[]{:S(2)}, u32[]{:S(2)}) %collective-permute-start.1) | collective-permute-done | bytes 2097184 | tf_op jit(solution)/shard_map/while/body/eval_jaxpr/ppermute | solution.py:10
  268.1 6.0 %fusion.26 = f32[1024,1024]{1,0:T(8,128)} fusion(bf16[1024,1024]{1,0:T(8,128)(2,1)} %get-tuple-element.353, bf16[1024,1024]{1,0:T(8,128)(2,1)S(1)} %collective-permute-done.1), kind=kOutput, calls=%fused_computation.10.clone.1 | convolution fusion | flops 2147483648 | bytes 8388608 | tf_op jit(solution)/shard_map/while/body/eval_jaxpr/dot_general | solution.py:28
  277.9 3.1 multiply_dynamic-update-slice_fusion.6
  281.0 7.9 %reduce-scatter.11.cloned.1.call-done = f32[512,1024]{1,0:T(8,128)} async-done(((f32[1024,1024]{1,0:T(8,128)}), f32[512,1024]{1,0:T(8,128)}) %reduce-scatter.11.cloned.1.call-update) | async-done | bytes 2097168 | tf_op jit(solution)/shard_map/while/body/eval_jaxpr/reduce_scatter | solution.py:31
  288.9 3.3 multiply_dynamic-update-slice_fusion.7
  292.2 1.4 collective-permute-start
  293.7 48.6 %collective-permute-done = bf16[1024,1024]{1,0:T(8,128)(2,1)S(1)} collective-permute-done((bf16[1024,1024]{1,0:T(8,128)(2,1)}, bf16[1024,1024]{1,0:T(8,128)(2,1)S(1)}, u32[]{:S(2)}, u32[]{:S(2)}) %collective-permute-start) | collective-permute-done | bytes 2097184 | tf_op jit(solution)/shard_map/while/body/eval_jaxpr/ppermute | solution.py:10
  342.3 5.9 %fusion.24 = f32[1024,1024]{1,0:T(8,128)} fusion(bf16[1024,1024]{1,0:T(8,128)(2,1)} %get-tuple-element.353, bf16[1024,1024]{1,0:T(8,128)(2,1)S(1)} %collective-permute-done), kind=kOutput, calls=%fused_computation.9.clone.1 | convolution fusion | flops 2147483648 | bytes 8388608 | tf_op jit(solution)/shard_map/while/body/eval_jaxpr/dot_general | solution.py:28
  349.6 45.1 %collective-permute-done.1 = bf16[1024,1024]{1,0:T(8,128)(2,1)S(1)} collective-permute-done((bf16[1024,1024]{1,0:T(8,128)(2,1)}, bf16[1024,1024]{1,0:T(8,128)(2,1)S(1)}, u32[]{:S(2)}, u32[]{:S(2)}) %collective-permute-start.1) | collective-permute-done | bytes 2097184 | tf_op jit(solution)/shard_map/while/body/eval_jaxpr/ppermute | solution.py:10
  396.1 6.0 %fusion.26 = f32[1024,1024]{1,0:T(8,128)} fusion(bf16[1024,1024]{1,0:T(8,128)(2,1)} %get-tuple-element.353, bf16[1024,1024]{1,0:T(8,128)(2,1)S(1)} %collective-permute-done.1), kind=kOutput, calls=%fused_computation.10.clone.1 | convolution fusion | flops 2147483648 | bytes 8388608 | tf_op jit(solution)/shard_map/while/body/eval_jaxpr/dot_general | solution.py:28
  405.8 3.1 multiply_dynamic-update-slice_fusion.6
  409.0 7.9 %reduce-scatter.11.cloned.1.call-done = f32[512,1024]{1,0:T(8,128)} async-done(((f32[1024,1024]{1,0:T(8,128)}), f32[512,1024]{1,0:T(8,128)}) %reduce-scatter.11.cloned.1.call-update) | async-done | bytes 2097168 | tf_op jit(solution)/shard_map/while/body/eval_jaxpr/reduce_scatter | solution.py:31
  416.9 3.3 multiply_dynamic-update-slice_fusion.7
  421.6 48.7 %collective-permute-done.2 = bf16[1024,1024]{1,0:T(8,128)(2,1)S(1)} collective-permute-done((bf16[1024,1024]{1,0:T(8,128)(2,1)}, bf16[1024,1024]{1,0:T(8,128)(2,1)S(1)}, u32[]{:S(2)}, u32[]{:S(2)}) %collective-permute-start.2) | collective-permute-done | bytes 2097184 | tf_op jit(solution)/shard_map/ppermute | solution.py:10
  470.3 4.4 convolution_bitcast_fusion
  474.7 11.3 %reduce-scatter.7.cloned.1.call-done = f32[512,1024]{1,0:T(8,128)} async-done(((f32[1024,1024]{1,0:T(8,128)}), f32[512,1024]{1,0:T(8,128)}) %reduce-scatter.7.cloned.1.call-update) | async-done | bytes 2097168 | tf_op jit(solution)/shard_map/reduce_scatter | solution.py:31
  486.0 3.1 multiply_dynamic-update-slice_fusion.2
  (65 shorter events, 26.4 us)
Async XLA Ops:
  6.5 21.4 %reduce-scatter.5.cloned.1.call-start = ((), (), s32[]{:S(2)}) async-start(), calls=%async_computation.4 | async-start | bytes 6291456 | tf_op jit(solution)/shard_map/reduce_scatter | solution.py:31
  13.2 1.6 copy-start.3
  16.1 1.3 copy-start.6
  28.0 2.0 copy-start.5
  30.2 6.2 %copy-start.2 = (f32[512,8192]{1,0:T(8,128)}, f32[512,8192]{1,0:T(8,128)S(1)}, u32[]{:S(2)}) copy-start(f32[512,8192]{1,0:T(8,128)S(1)} %multiply_dynamic-update-slice_fusion.3) | copy-start | bytes 50331652
  36.4 113.6 %reduce-scatter.9.cloned.1.call-start = ((), (), s32[]{:S(2)}) async-start(), calls=%async_computation.6 | async-start | bytes 6291456 | tf_op jit(solution)/shard_map/while/body/eval_jaxpr/reduce_scatter | solution.py:31
  36.4 50.1 %collective-permute-start = (bf16[1024,1024]{1,0:T(8,128)(2,1)}, bf16[1024,1024]{1,0:T(8,128)(2,1)S(1)}, u32[]{:S(2)}, u32[]{:S(2)}) collective-permute-start(bf16[1024,1024]{1,0:T(8,128)(2,1)} %get-tuple-element.298), channel_id=1, source_target_pairs={{0,2},{2,4},{4,6},{6,8},{8,10},{10,12},{12,14},{14,0},{1,3},{3,5},... | collective-permute-start | bytes 6291464 | tf_op jit(solution)/shard_map/while/body/eval_jaxpr/ppermute | solution.py:10
  92.4 68.6 %reduce-scatter.11.cloned.1.call-start = ((), (), s32[]{:S(2)}) async-start(), calls=%async_computation.7 | async-start | bytes 6291456 | tf_op jit(solution)/shard_map/while/body/eval_jaxpr/reduce_scatter | solution.py:31
  92.5 46.5 %collective-permute-start.1 = (bf16[1024,1024]{1,0:T(8,128)(2,1)}, bf16[1024,1024]{1,0:T(8,128)(2,1)S(1)}, u32[]{:S(2)}, u32[]{:S(2)}) collective-permute-start(bf16[1024,1024]{1,0:T(8,128)(2,1)} %get-tuple-element.299), channel_id=1, source_target_pairs={{0,14},{2,0},{4,2},{6,4},{8,6},{10,8},{12,10},{14,12},{1,15},{3,1}... | collective-permute-start | bytes 6291464 | tf_op jit(solution)/shard_map/while/body/eval_jaxpr/ppermute | solution.py:10
  139.0 1.3 copy-start
  146.4 2.3 copy-start.1
  161.0 3.3 copy-start.4
  164.3 113.5 %reduce-scatter.9.cloned.1.call-start = ((), (), s32[]{:S(2)}) async-start(), calls=%async_computation.6 | async-start | bytes 6291456 | tf_op jit(solution)/shard_map/while/body/eval_jaxpr/reduce_scatter | solution.py:31
  164.3 50.0 %collective-permute-start = (bf16[1024,1024]{1,0:T(8,128)(2,1)}, bf16[1024,1024]{1,0:T(8,128)(2,1)S(1)}, u32[]{:S(2)}, u32[]{:S(2)}) collective-permute-start(bf16[1024,1024]{1,0:T(8,128)(2,1)} %get-tuple-element.298), channel_id=1, source_target_pairs={{0,2},{2,4},{4,6},{6,8},{8,10},{10,12},{12,14},{14,0},{1,3},{3,5},... | collective-permute-start | bytes 6291464 | tf_op jit(solution)/shard_map/while/body/eval_jaxpr/ppermute | solution.py:10
  220.3 68.6 %reduce-scatter.11.cloned.1.call-start = ((), (), s32[]{:S(2)}) async-start(), calls=%async_computation.7 | async-start | bytes 6291456 | tf_op jit(solution)/shard_map/while/body/eval_jaxpr/reduce_scatter | solution.py:31
  220.4 46.5 %collective-permute-start.1 = (bf16[1024,1024]{1,0:T(8,128)(2,1)}, bf16[1024,1024]{1,0:T(8,128)(2,1)S(1)}, u32[]{:S(2)}, u32[]{:S(2)}) collective-permute-start(bf16[1024,1024]{1,0:T(8,128)(2,1)} %get-tuple-element.299), channel_id=1, source_target_pairs={{0,14},{2,0},{4,2},{6,4},{8,6},{10,8},{12,10},{14,12},{1,15},{3,1}... | collective-permute-start | bytes 6291464 | tf_op jit(solution)/shard_map/while/body/eval_jaxpr/ppermute | solution.py:10
  266.8 1.3 copy-start
  274.2 2.3 copy-start.1
  288.9 3.3 copy-start.4
  292.2 113.6 %reduce-scatter.9.cloned.1.call-start = ((), (), s32[]{:S(2)}) async-start(), calls=%async_computation.6 | async-start | bytes 6291456 | tf_op jit(solution)/shard_map/while/body/eval_jaxpr/reduce_scatter | solution.py:31
  292.2 50.1 %collective-permute-start = (bf16[1024,1024]{1,0:T(8,128)(2,1)}, bf16[1024,1024]{1,0:T(8,128)(2,1)S(1)}, u32[]{:S(2)}, u32[]{:S(2)}) collective-permute-start(bf16[1024,1024]{1,0:T(8,128)(2,1)} %get-tuple-element.298), channel_id=1, source_target_pairs={{0,2},{2,4},{4,6},{6,8},{8,10},{10,12},{12,14},{14,0},{1,3},{3,5},... | collective-permute-start | bytes 6291464 | tf_op jit(solution)/shard_map/while/body/eval_jaxpr/ppermute | solution.py:10
  348.3 68.6 %reduce-scatter.11.cloned.1.call-start = ((), (), s32[]{:S(2)}) async-start(), calls=%async_computation.7 | async-start | bytes 6291456 | tf_op jit(solution)/shard_map/while/body/eval_jaxpr/reduce_scatter | solution.py:31
  348.3 46.5 %collective-permute-start.1 = (bf16[1024,1024]{1,0:T(8,128)(2,1)}, bf16[1024,1024]{1,0:T(8,128)(2,1)S(1)}, u32[]{:S(2)}, u32[]{:S(2)}) collective-permute-start(bf16[1024,1024]{1,0:T(8,128)(2,1)} %get-tuple-element.299), channel_id=1, source_target_pairs={{0,14},{2,0},{4,2},{6,4},{8,6},{10,8},{12,10},{14,12},{1,15},{3,1}... | collective-permute-start | bytes 6291464 | tf_op jit(solution)/shard_map/while/body/eval_jaxpr/ppermute | solution.py:10
  394.8 1.3 copy-start
  402.2 2.3 copy-start.1
  416.9 3.3 copy-start.4
  420.2 65.8 %reduce-scatter.7.cloned.1.call-start = ((), (), s32[]{:S(2)}) async-start(), calls=%async_computation.5 | async-start | bytes 6291456 | tf_op jit(solution)/shard_map/reduce_scatter | solution.py:31
  420.2 50.1 %collective-permute-start.2 = (bf16[1024,1024]{1,0:T(8,128)(2,1)}, bf16[1024,1024]{1,0:T(8,128)(2,1)S(1)}, u32[]{:S(2)}, u32[]{:S(2)}) collective-permute-start(bf16[1024,1024]{1,0:T(8,128)(2,1)} %get-tuple-element.340), channel_id=1, source_target_pairs={{0,2},{2,4},{4,6},{6,8},{8,10},{10,12},{12,14},{14,0},{1,3},{3,5},... | collective-permute-start | bytes 6291464 | tf_op jit(solution)/shard_map/ppermute | solution.py:10
Sparse Core Ops, SparseCore 0:
  13.3 14.6 reduce-scatter.4
  92.6 11.1 reduce-scatter.8
  146.4 14.5 reduce-scatter.10
  220.4 11.2 reduce-scatter.8
  274.3 14.5 reduce-scatter.10
  348.4 11.1 reduce-scatter.8
  402.2 14.6 reduce-scatter.10
  474.8 11.1 reduce-scatter.6
where the time goes:
time: 497 us; the launch traced here: 496 us
  waiting for transfers between devices  376 us (76%)
  matrix products  46.7 us (9%)
  local copies, waits for them, and re-layouts  27.3 us (5%)
  other arithmetic  22.8 us (5%)
  between operations  13.5 us (3%)
  starting transfers between devices  9.78 us (2%)
    ppermute x7, waiting for transfers between devices, from_behind(): return lax.ppermute(value, axis, pairs)  330 us
    dot_general x8, matrix products, tile_of(): lax.dot_general(interactions, panel_data, contract, preferred_element_typ...  46.7 us
    reduce_scatter x8, waiting for transfers between devices, tile_of(): return lax.psum_scatter(full_tile, 'user', scatter_dimension=0, tiled=True)  45.5 us
    dynamic_update_slice x8, other arithmetic, place_tile(): lax.dynamic_update_slice_in_dim(result, scaled, source * block_items, 1)  22.7 us
    while x24, local copies, waits for them, and re-layouts  14.8 us
    unnamed x10, local copies, waits for them, and re-layouts  10.3 us
  transfers between devices with their start and end apart: 15, of which 12 were waited for; matrix products, arithmetic and copies ran while one was open for 8% of the time, Pallas kernels for 0%

commit v1 on v0

v1 whole, which is shorter than its diff:
```python
import functools

import jax
import jax.numpy as jnp
from jax import lax
from jax.experimental import pallas as pl
from jax.experimental.pallas import tpu as pltpu
from jax.sharding import PartitionSpec as P

MESH = pl.DeviceIdType.MESH
PIECES = 4


def kernel(nz, ny, x_ref, row_ref, col_ref, out_ref, panel, left, made,
           got, got_core, sent_down, sent_up, sent_side, sent_core, placed, loaded):
    users, block = x_ref.shape
    half = out_ref.shape[0]
    rows = users // PIECES
    split = PIECES // 2
    group = lax.axis_index("groups")
    me = lax.axis_index("item")
    core = lax.axis_index("user")
    z, y = me // ny, me % ny
    base = core * users

    def at(zz, yy):
        return (group, zz * ny + yy, core)

    down, up, side = at(z - 1, y), at(z + 1, y), at(z, ny - 1 - y)
    other = (group, me, 1 - core)
    not_first, not_last = z > 0, z < nz - 1

    barrier = pltpu.get_barrier_semaphore()
    pl.semaphore_signal(barrier, inc=1, device_id=other, device_id_type=MESH)
    if ny > 1:
        pl.semaphore_signal(barrier, inc=1, device_id=side, device_id_type=MESH)

    @pl.when(not_first)
    def _():
        pl.semaphore_signal(barrier, inc=1, device_id=down, device_id_type=MESH)

    @pl.when(not_last)
    def _():
        pl.semaphore_signal(barrier, inc=1, device_id=up, device_id_type=MESH)

    load = pltpu.make_async_copy(x_ref, panel.at[me, pl.ds(base, users)], loaded)
    load.start()
    wanted = ny + jnp.where(not_first, 1, 0) + jnp.where(not_last, 1, 0)
    pl.semaphore_wait(barrier, wanted)

    def place(b, p):
        return panel.at[b, pl.ds(pl.multiple_of(base + p * rows, rows), rows)]

    def send(b, p, sems, recv, device, source=None):
        pltpu.make_async_remote_copy(
            src_ref=place(b, p) if source is None else source,
            dst_ref=place(b, p),
            send_sem=sems.at[b],
            recv_sem=recv,
            device_id=device,
            device_id_type=MESH,
        ).start()

    def take(b, p):
        pltpu.make_async_copy(place(b, p), place(b, p), got.at[b, p]).wait()

    def to_down(b, p, source=None):
        @pl.when(not_first)
        def _():
            send(b, p, sent_down, got.at[b, p], down, source)

    def to_up(b, p, source=None):
        @pl.when(not_last)
        def _():
            send(b, p, sent_up, got.at[b, p], up, source)

    def to_side(b, p, source=None):
        send(b, p, sent_side, got.at[b, p], side, source)

    def to_core(b, p, source=None):
        send(b, p, sent_core, got_core.at[b], other, source)

    for p in range(PIECES):
        mine = x_ref.at[pl.ds(p * rows, rows)]
        to_down(me, p, mine)
        to_up(me, p, mine)
        if ny > 1:
            to_side(me, p, mine)
        to_core(me, p, mine)

    def whole(b, sem, start, count):
        piece = panel.at[b, pl.ds(start, count)]
        pltpu.make_async_copy(piece, piece, sem).wait()

    def take_core(b):
        whole(b, got_core.at[b], (1 - core) * users, users)

    tile = min(256, block)

    def product(b):
        def columns(c, _):
            cols = pl.ds(pl.multiple_of(c * tile, tile), tile)
            co = jnp.dot(left[...], panel[b, :, cols], preferred_element_type=jnp.float32)
            made[b, :, cols] = co * row_ref[...] * col_ref[b, :, cols]
            return 0

        lax.fori_loop(0, block // tile, columns, 0)
        result(b).start()

    def result(b):
        return pltpu.make_async_copy(
            made.at[b], out_ref.at[:, pl.ds(pl.multiple_of(b * block, block), block)], placed.at[b])

    load.wait()
    take_core(me)
    quarter = min(256, users)

    def turn(c, _):
        part = pl.ds(pl.multiple_of(c * quarter, quarter), quarter)
        own = panel[me, part, pl.ds(pl.multiple_of(core * half, half), half)]
        left[:, part] = own.astype(jnp.float32).T.astype(left.dtype)
        return 0

    lax.fori_loop(0, 2 * users // quarter, turn, 0)
    product(me)

    def step(s, _):
        t, p = s // PIECES, s % PIECES

        def along(zb, onward):
            b = zb * ny + y

            @pl.when(jnp.logical_and(zb >= 0, zb < nz))
            def _():
                take(b, p)
                onward(b, p)
                if ny > 1:
                    @pl.when(jnp.logical_or(t > 0, p >= split))
                    def _():
                        to_side(b, p)
                to_core(b, p)

        along(z + 1 + t, to_down)
        along(z - 1 - t, to_up)
        if ny > 1:
            b0 = z * ny + (ny - 1 - y)

            @pl.when(t == 0)
            def _():
                take(b0, p)

                @pl.when(p < split)
                def _():
                    to_down(b0, p)
                    to_up(b0, p)

                to_core(b0, p)

            def crossed(zb):
                @pl.when(jnp.logical_and(t > 0, jnp.logical_and(zb >= 0, zb < nz)))
                def _():
                    b = zb * ny + (ny - 1 - y)
                    take(b, p)
                    to_core(b, p)

            crossed(z + t)
            crossed(z - t)

        kinds = 4 if ny > 1 else 2
        tt = t - 1
        back, crossing = p % 2, p // 2
        zb = z + (1 - 2 * back) * (tt + 1 - crossing)
        yb = y + crossing * (ny - 1 - 2 * y)
        fits = jnp.logical_and(zb >= 0, zb < nz)
        first = jnp.logical_and(p < kinds, jnp.logical_or(tt > 0, jnp.logical_and(tt == 0, p < 3)))

        @pl.when(jnp.logical_and(fits, first))
        def _():
            b = zb * ny + yb
            take_core(b)
            product(b)

        return 0

    lax.fori_loop(0, (nz + 1) * PIECES, step, 0)

    def drain(b, _):
        zb, yb = b // ny, b % ny
        result(b).wait()
        whole(b, sent_core.at[b], base, users)
        straight = yb == y

        @pl.when(jnp.logical_and(straight, jnp.logical_and(zb >= z, not_first)))
        def _():
            whole(b, sent_down.at[b], base, users)

        @pl.when(jnp.logical_and(straight, jnp.logical_and(zb <= z, not_last)))
        def _():
            whole(b, sent_up.at[b], base, users)

        if ny > 1:
            layer = jnp.logical_and(jnp.logical_not(straight), zb == z)
            near = jnp.logical_or(zb == z + 1, zb == z - 1)

            @pl.when(jnp.logical_and(layer, not_first))
            def _():
                whole(b, sent_down.at[b], base, split * rows)

            @pl.when(jnp.logical_and(layer, not_last))
            def _():
                whole(b, sent_up.at[b], base, split * rows)

            @pl.when(jnp.logical_and(straight, near))
            def _():
                whole(b, sent_side.at[b], base, (PIECES - split) * rows)

            @pl.when(jnp.logical_and(straight, jnp.logical_not(near)))
            def _():
                whole(b, sent_side.at[b], base, users)

        return 0

    lax.fori_loop(0, nz * ny, drain, 0)


def shards(nz, ny, interactions, counts):
    users, block = interactions.shape
    n = nz * ny
    half = block // lax.axis_size("user")
    count_float = counts.astype(jnp.float32)
    start = lax.axis_index("item") * block + lax.axis_index("user") * half
    row_damp = (lax.dynamic_slice_in_dim(count_float, start, half) ** (-0.4))[:, None]
    col_damp = (count_float ** (-0.6)).reshape(n, 1, block)
    dma = pltpu.SemaphoreType.DMA
    return pl.pallas_call(
        functools.partial(kernel, nz, ny),
        out_shape=jax.ShapeDtypeStruct((half, n * block), jnp.float32),
        in_specs=[
            pl.BlockSpec(memory_space=pl.ANY),
            pl.BlockSpec(memory_space=pltpu.VMEM),
            pl.BlockSpec(memory_space=pltpu.VMEM),
        ],
        out_specs=pl.BlockSpec(memory_space=pl.ANY),
        scratch_shapes=[
            pltpu.VMEM((n, 2 * users, block), interactions.dtype),
            pltpu.VMEM((half, 2 * users), interactions.dtype),
            pltpu.VMEM((n, half, block), jnp.float32),
            dma((n, PIECES)),
            dma((n,)),
            dma((n,)),
            dma((n,)),
            dma((n,)),
            dma((n,)),
            dma((n,)),
            dma,
        ],
        compiler_params=pltpu.CompilerParams(
            collective_id=0, has_side_effects=True, vmem_limit_bytes=60 * 1024 * 1024
        ),
        cost_estimate=pl.CostEstimate(
            flops=4 * half * users * n * block, bytes_accessed=4 * half * n * block, transcendentals=0
        ),
    )(interactions, row_damp, col_damp)


def columns_of(mesh):
    n = mesh.shape["item"]
    spots = [getattr(d, "coords", None) for d in mesh.devices[0, :, 0]]
    if any(spot is None for spot in spots):
        return 1
    ny = len({spot[1] for spot in spots})
    return ny if ny == 2 and n % 2 == 0 else 1


def solution(mesh):
    ny = columns_of(mesh)
    placed = (P(("groups", "user"), "item"), P("groups"))
    return jax.shard_map(
        functools.partial(shards, mesh.shape["item"] // ny, ny),
        mesh=mesh,
        in_specs=placed,
        out_specs=P(("groups", "item", "user"), None),
        check_vma=False,
    )
```

time: 497 us -> 198 us (0.40)
  waiting for transfers between devices: 376 us -> 0 us
  Pallas kernels: 0 us -> 182 us
  matrix products: 46.7 us -> 0 us
  other arithmetic: 22.8 us -> 2.14 us
  local copies, waits for them, and re-layouts: 27.3 us -> 12.6 us
  between operations: 13.5 us -> 0.01 us
  starting transfers between devices: 9.78 us -> 0 us
    ppermute x7 -> x0, waiting for transfers between devices: 330 us -> none  [from_behind(): return lax.ppermute(value, axis, pairs)]
    pallas_call x0 -> x1, Pallas kernels: none -> 182 us  [shards(): pl.pallas_call(functools.partial(kernel, nz, ny), out_shape=jax.ShapeDtyp...]
    dot_general x8 -> x0, matrix products: 46.7 us -> none  [tile_of(): lax.dot_general(interactions, panel_data, contract, preferred_element_typ...]
    reduce_scatter x8 -> x0, waiting for transfers between devices: 45.5 us -> none  [tile_of(): return lax.psum_scatter(full_tile, 'user', scatter_dimension=0, tiled=True)]
    dynamic_update_slice x8 -> x0, other arithmetic: 22.7 us -> none  [place_tile(): lax.dynamic_update_slice_in_dim(result, scaled, source * block_items, 1)]
    while x24 -> x0, local copies, waits for them, and re-layouts: 14.8 us -> none
    ppermute x7 -> x0, starting transfers between devices: 9.65 us -> none  [from_behind(): return lax.ppermute(value, axis, pairs)]
    unnamed x10 -> x1, local copies, waits for them, and re-layouts: 10.3 us -> 11.7 us
  transfers between devices with their start and end apart: 15 -> 0, of which waited for: 12 -> 0; matrix products, arithmetic and copies ran while one was open for 8% -> 0% of each run, Pallas kernels for 0% -> 0%
where the time goes in v1:
time: 198 us; the launch traced here: 197 us
  Pallas kernels  182 us (92%)
  local copies, waits for them, and re-layouts  12.6 us (6%)
  other arithmetic  2.14 us (1%)
    pallas_call x1, Pallas kernels, shards(): pl.pallas_call(functools.partial(kernel, nz, ny), out_shape=jax.ShapeDtyp...  182 us
    unnamed x1, local copies, waits for them, and re-layouts  11.7 us

profile of v1, /device:TPU:1, one launch (start us, length us, event | category | flops | bytes accessed | tf_op | source)
XLA Modules:
  0.0 197.2 jit_solution(896027134709427119)
XLA Ops:
  0.0 1.4 broadcast_power_fusion
  1.4 0.8 convert_element_type.3
  2.1 0.1 dynamic-slice_power_fusion
  2.2 0.9 copy.3.row_ref
  3.1 182.5 %shard_map.28 = f32[512,8192]{1,0:T(8,128)} custom-call(bf16[1024,1024]{1,0:T(8,128)(2,1)} %x_ref.1, f32[512,1]{1,0:T(8,128)} %copy.3.row_ref, f32[8,1,1024]{2,1,0:T(1,128)} %bitcast.2), custom_call_target="tpu_custom_call" | custom-call | flops 17179869184 | bytes 16777216 | tf_op jit(solution)/shard_map/pallas_call | solution.py:235
  185.6 11.7 %copy.5 = f32[512,8192]{1,0:T(8,128)} copy(f32[512,8192]{1,0:T(8,128)} %shard_map.28) | data formatting | bytes 33554432

commit v2 on v1

--- a/solution.py
+++ b/solution.py
@@ -8,11 +8,11 @@
 from jax.sharding import PartitionSpec as P
 
 MESH = pl.DeviceIdType.MESH
-PIECES = 4
-
-
-def kernel(nz, ny, x_ref, row_ref, col_ref, out_ref, panel, left, made,
-           got, got_core, sent_down, sent_up, sent_side, sent_core, placed, loaded):
+PIECES = 8
+
+
+def kernel(nz, ny, x_ref, counts_ref, out_ref, panel, left, row_damp, col_damp,
+           got, got_core, sent_down, sent_up, sent_side, sent_core, loaded):
     users, block = x_ref.shape
     half = out_ref.shape[0]
     rows = users // PIECES
@@ -101,16 +101,16 @@
         def columns(c, _):
             cols = pl.ds(pl.multiple_of(c * tile, tile), tile)
             co = jnp.dot(left[...], panel[b, :, cols], preferred_element_type=jnp.float32)
-            made[b, :, cols] = co * row_ref[...] * col_ref[b, :, cols]
+            spot = pl.ds(pl.multiple_of(b * block + c * tile, tile), tile)
+            out_ref[:, spot] = co * row_damp[:, :1] * col_damp[b, :, cols]
             return 0
 
         lax.fori_loop(0, block // tile, columns, 0)
-        result(b).start()
-
-    def result(b):
-        return pltpu.make_async_copy(
-            made.at[b], out_ref.at[:, pl.ds(pl.multiple_of(b * block, block), block)], placed.at[b])
-
+
+    logs = jnp.log(counts_ref[...].astype(jnp.float32))
+    col_damp[...] = jnp.exp(-0.6 * logs)
+    mine = counts_ref[me, :, pl.ds(pl.multiple_of(core * half, half), half)].astype(jnp.float32)
+    row_damp[...] = jnp.broadcast_to(jnp.exp(-0.4 * jnp.log(mine)), (128, half)).T
     load.wait()
     take_core(me)
     quarter = min(256, users)
@@ -168,11 +168,13 @@
 
         kinds = 4 if ny > 1 else 2
         tt = t - 1
-        back, crossing = p % 2, p // 2
+        kind = p // (PIECES // 4)
+        back, crossing = kind % 2, kind // 2
         zb = z + (1 - 2 * back) * (tt + 1 - crossing)
         yb = y + crossing * (ny - 1 - 2 * y)
         fits = jnp.logical_and(zb >= 0, zb < nz)
-        first = jnp.logical_and(p < kinds, jnp.logical_or(tt > 0, jnp.logical_and(tt == 0, p < 3)))
+        turn_now = jnp.logical_and(p % (PIECES // 4) == 0, kind < kinds)
+        first = jnp.logical_and(turn_now, jnp.logical_or(tt > 0, jnp.logical_and(tt == 0, kind < 3)))
 
         @pl.when(jnp.logical_and(fits, first))
         def _():
@@ -186,7 +188,6 @@
 
     def drain(b, _):
         zb, yb = b // ny, b % ny
-        result(b).wait()
         whole(b, sent_core.at[b], base, users)
         straight = yb == y
 
@@ -227,26 +228,21 @@
     users, block = interactions.shape
     n = nz * ny
     half = block // lax.axis_size("user")
-    count_float = counts.astype(jnp.float32)
-    start = lax.axis_index("item") * block + lax.axis_index("user") * half
-    row_damp = (lax.dynamic_slice_in_dim(count_float, start, half) ** (-0.4))[:, None]
-    col_damp = (count_float ** (-0.6)).reshape(n, 1, block)
     dma = pltpu.SemaphoreType.DMA
     return pl.pallas_call(
         functools.partial(kernel, nz, ny),
-        out_shape=jax.ShapeDtypeStruct((half, n * block), jnp.float32),
+        out_shape=pltpu.VMEM((half, n * block), jnp.float32),
         in_specs=[
             pl.BlockSpec(memory_space=pl.ANY),
             pl.BlockSpec(memory_space=pltpu.VMEM),
-            pl.BlockSpec(memory_space=pltpu.VMEM),
         ],
-        out_specs=pl.BlockSpec(memory_space=pl.ANY),
+        out_specs=pl.BlockSpec(memory_space=pltpu.VMEM),
         scratch_shapes=[
             pltpu.VMEM((n, 2 * users, block), interactions.dtype),
             pltpu.VMEM((half, 2 * users), interactions.dtype),
-            pltpu.VMEM((n, half, block), jnp.float32),
+            pltpu.VMEM((half, 128), jnp.float32),
+            pltpu.VMEM((n, 1, block), jnp.float32),
             dma((n, PIECES)),
-            dma((n,)),
             dma((n,)),
             dma((n,)),
             dma((n,)),
@@ -255,12 +251,12 @@
             dma,
         ],
         compiler_params=pltpu.CompilerParams(
-            collective_id=0, has_side_effects=True, vmem_limit_bytes=60 * 1024 * 1024
+            collective_id=0, has_side_effects=True, vmem_limit_bytes=40 * 1024 * 1024
         ),
         cost_estimate=pl.CostEstimate(
             flops=4 * half * users * n * block, bytes_accessed=4 * half * n * block, transcendentals=0
         ),
-    )(interactions, row_damp, col_damp)
+    )(interactions, counts.reshape(n, 1, block))
 
 
 def columns_of(mesh):

time: 198 us -> 184 us (0.929)
  local copies, waits for them, and re-layouts: 12.6 us -> 6.16 us
  Pallas kernels: 182 us -> 176 us
  other arithmetic: 2.14 us -> 0 us
    pallas_call x1, Pallas kernels: 182 us -> 176 us  [shards(): pl.pallas_call(functools.partial(kernel, nz, ny), out_shape=pltpu.VMEM((h...]
    unnamed x1, local copies, waits for them, and re-layouts: 11.7 us -> 6.16 us
where the time goes in v2:
time: 184 us; the launch traced here: 183 us
  Pallas kernels  176 us (96%)
  local copies, waits for them, and re-layouts  6.16 us (3%)
    pallas_call x1, Pallas kernels, shards(): pl.pallas_call(functools.partial(kernel, nz, ny), out_shape=pltpu.VMEM((h...  176 us
    unnamed x1, local copies, waits for them, and re-layouts  6.16 us

profile of v2, /device:TPU:1, one launch (start us, length us, event | category | flops | bytes accessed | tf_op | source)
XLA Modules:
  0.0 182.6 jit_solution(8186279882299820411)
XLA Ops:
  0.0 176.5 %shard_map.28 = f32[512,8192]{1,0:T(8,128)S(1)} custom-call(bf16[1024,1024]{1,0:T(8,128)(2,1)} %x_ref.1, s32[8,1,1024]{2,1,0:T(1,128)} %bitcast.1), custom_call_target="tpu_custom_call" | custom-call | flops 17179869184 | bytes 16777216 | tf_op jit(solution)/shard_map/pallas_call | solution.py:232
  176.5 6.2 %copy.4 = f32[512,8192]{1,0:T(8,128)} copy(f32[512,8192]{1,0:T(8,128)S(1)} %shard_map.28) | data formatting | bytes 33554432

commit v3 on v2

--- a/solution.py
+++ b/solution.py
@@ -9,10 +9,15 @@
 
 MESH = pl.DeviceIdType.MESH
 PIECES = 8
+LEVELS = 32767
+
+
+def has_far(nz, ny):
+    return nz == 4 and ny == 2
 
 
 def kernel(nz, ny, x_ref, counts_ref, out_ref, panel, left, row_damp, col_damp,
-           got, got_core, sent_down, sent_up, sent_side, sent_core, loaded):
+           got, got_core, sent_down, sent_up, sent_side, sent_core, loaded, *remote):
     users, block = x_ref.shape
     half = out_ref.shape[0]
     rows = users // PIECES
@@ -29,6 +34,14 @@
     down, up, side = at(z - 1, y), at(z + 1, y), at(z, ny - 1 - y)
     other = (group, me, 1 - core)
     not_first, not_last = z > 0, z < nz - 1
+    far = has_far(nz, ny)
+    reach = nz - 2 if far else nz - 1
+    is_end = jnp.logical_or(z == 0, z == nz - 1)
+    is_middle = jnp.logical_not(is_end)
+    near_end = jnp.where(z < 2, 0, nz - 1)
+    far_end = nz - 1 - near_end
+    if far:
+        left_far, sums, scales, sent_sums, got_sums, sent_scales, got_scales = remote
 
     barrier = pltpu.get_barrier_semaphore()
     pl.semaphore_signal(barrier, inc=1, device_id=other, device_id_type=MESH)
@@ -115,14 +128,77 @@
     take_core(me)
     quarter = min(256, users)
 
-    def turn(c, _):
-        part = pl.ds(pl.multiple_of(c * quarter, quarter), quarter)
-        own = panel[me, part, pl.ds(pl.multiple_of(core * half, half), half)]
-        left[:, part] = own.astype(jnp.float32).T.astype(left.dtype)
+    def turned(b, target):
+        def turn(c, _):
+            part = pl.ds(pl.multiple_of(c * quarter, quarter), quarter)
+            own = panel[b, part, pl.ds(pl.multiple_of(core * half, half), half)]
+            target[:, part] = own.astype(jnp.float32).T.astype(target.dtype)
+            return 0
+
+        lax.fori_loop(0, 2 * users // quarter, turn, 0)
+
+    turned(me, left)
+    product(me)
+    tiles = block // tile
+
+    def far_block(k):
+        return far_end * ny + y + k * (ny - 1 - 2 * y)
+
+    def sums_copy(k, c):
+        return pltpu.make_async_remote_copy(
+            src_ref=sums.at[k, c], dst_ref=sums.at[k, c], send_sem=sent_sums.at[k], recv_sem=got_sums.at[k],
+            device_id=at(near_end, y), device_id_type=MESH)
+
+    def scales_copy(k):
+        return pltpu.make_async_remote_copy(
+            src_ref=scales.at[k], dst_ref=scales.at[k], send_sem=sent_scales.at[k], recv_sem=got_scales.at[k],
+            device_id=at(near_end, y), device_id_type=MESH)
+
+    def send_sums(k, _):
+        b = far_block(k)
+        take_core(b)
+        scales[k] = jnp.zeros((8, half), jnp.float32)
+
+        def columns(c, _):
+            cols = pl.ds(pl.multiple_of(c * tile, tile), tile)
+            co = jnp.dot(left_far[...], panel[b, :, cols], preferred_element_type=jnp.float32)
+            most = jnp.maximum(jnp.max(co, axis=1, keepdims=True), 1e-30)
+            level = (co * (2 * LEVELS / most) + 0.5).astype(jnp.int32) - LEVELS
+            sums[k, c] = level.astype(jnp.int16)
+            unit = jnp.broadcast_to(most * (0.5 / LEVELS), (half, 128)).T
+            scales[k, pl.ds(c, 1), :] = unit[0:1]
+            sums_copy(k, c).start()
+            return 0
+
+        lax.fori_loop(0, tiles, columns, 0)
+        scales_copy(k).start()
         return 0
 
-    lax.fori_loop(0, 2 * users // quarter, turn, 0)
-    product(me)
+    def take_sums(k, _):
+        b = far_end_of_end() * ny + y + k * (ny - 1 - 2 * y)
+        pltpu.make_async_copy(sums.at[k], sums.at[k], got_sums.at[k]).wait()
+        pltpu.make_async_copy(scales.at[k], scales.at[k], got_scales.at[k]).wait()
+
+        def columns(c, _):
+            cols = pl.ds(pl.multiple_of(c * tile, tile), tile)
+            unit = jnp.broadcast_to(scales[k, pl.ds(c, 1), :], (128, half)).T
+            level = sums[k, c].astype(jnp.int32) + LEVELS
+            co = level.astype(jnp.float32) * unit[:, :1]
+            spot = pl.ds(pl.multiple_of(b * block + c * tile, tile), tile)
+            out_ref[:, spot] = co * row_damp[:, :1] * col_damp[b, :, cols]
+            return 0
+
+        lax.fori_loop(0, tiles, columns, 0)
+        return 0
+
+    def far_end_of_end():
+        return nz - 1 - z
+
+    def distance(t):
+        return jnp.where(is_middle, 3 - t, t) if far else t
+
+    def reached(t):
+        return jnp.logical_and(t >= 1, t <= reach)
 
     def step(s, _):
         t, p = s // PIECES, s % PIECES
@@ -130,12 +206,18 @@
         def along(zb, onward):
             b = zb * ny + y
 
-            @pl.when(jnp.logical_and(zb >= 0, zb < nz))
+            @pl.when(jnp.logical_and(t < reach, jnp.logical_and(zb >= 0, zb < nz)))
             def _():
                 take(b, p)
-                onward(b, p)
+
+                @pl.when(t + 2 <= reach)
+                def _():
+                    onward(b, p)
+
                 if ny > 1:
-                    @pl.when(jnp.logical_or(t > 0, p >= split))
+                    across = jnp.logical_or(t > 0, is_end if far else p >= split)
+
+                    @pl.when(across)
                     def _():
                         to_side(b, p)
                 to_core(b, p)
@@ -149,57 +231,134 @@
             def _():
                 take(b0, p)
 
-                @pl.when(p < split)
+                if not far:
+                    @pl.when(p < split)
+                    def _():
+                        to_down(b0, p)
+                        to_up(b0, p)
+
+                to_core(b0, p)
+
+            if far:
+                @pl.when(jnp.logical_and(s == PIECES, is_middle))
                 def _():
-                    to_down(b0, p)
-                    to_up(b0, p)
-
-                to_core(b0, p)
+                    def inward(q, _):
+                        @pl.when(z == 1)
+                        def _():
+                            to_up(b0, q)
+
+                        @pl.when(z == 2)
+                        def _():
+                            to_down(b0, q)
+
+                        return 0
+
+                    lax.fori_loop(0, PIECES, inward, 0)
+
+                @pl.when(jnp.logical_and(s == 2 * PIECES - 1, is_middle))
+                def _():
+                    def late(q, _):
+                        to_side(near_end * ny + y, q)
+                        return 0
+
+                    lax.fori_loop(0, PIECES, late, 0)
+
+            lag = 1 if far else 0
+            tc, pc = (s + PIECES - lag) // PIECES - 1, (s + PIECES - lag) % PIECES
 
             def crossed(zb):
-                @pl.when(jnp.logical_and(t > 0, jnp.logical_and(zb >= 0, zb < nz)))
+                @pl.when(jnp.logical_and(reached(tc), jnp.logical_and(zb >= 0, zb < nz)))
                 def _():
                     b = zb * ny + (ny - 1 - y)
-                    take(b, p)
-                    to_core(b, p)
-
-            crossed(z + t)
-            crossed(z - t)
+                    take(b, pc)
+                    to_core(b, pc)
+
+            crossed(z + distance(tc))
+            crossed(z - distance(tc))
+
+        if far:
+            @pl.when(jnp.logical_and(s == 2 * PIECES - 2, is_middle))
+            def _():
+                turned(near_end * ny + y, left_far)
+
+            @pl.when(jnp.logical_and(s == 2 * PIECES, is_middle))
+            def _():
+                lax.fori_loop(0, 2, send_sums, 0)
 
         kinds = 4 if ny > 1 else 2
         tt = t - 1
         kind = p // (PIECES // 4)
         back, crossing = kind % 2, kind // 2
-        zb = z + (1 - 2 * back) * (tt + 1 - crossing)
+        gap = jnp.where(crossing == 1, jnp.where(tt == 0, 0, distance(tt)), tt + 1)
+        zb = z + (1 - 2 * back) * gap
         yb = y + crossing * (ny - 1 - 2 * y)
-        fits = jnp.logical_and(zb >= 0, zb < nz)
+        fits = jnp.logical_and(jnp.logical_and(zb >= 0, zb < nz), jnp.logical_and(gap <= reach, tt <= reach))
         turn_now = jnp.logical_and(p % (PIECES // 4) == 0, kind < kinds)
         first = jnp.logical_and(turn_now, jnp.logical_or(tt > 0, jnp.logical_and(tt == 0, kind < 3)))
 
         @pl.when(jnp.logical_and(fits, first))
         def _():
             b = zb * ny + yb
-            take_core(b)
+            if far:
+                @pl.when(jnp.logical_or(is_end, tt != 1))
+                def _():
+                    take_core(b)
+            else:
+                take_core(b)
             product(b)
 
         return 0
 
-    lax.fori_loop(0, (nz + 1) * PIECES, step, 0)
+    lax.fori_loop(0, (reach + 2) * PIECES, step, 0)
+    if far:
+        @pl.when(is_end)
+        def _():
+            lax.fori_loop(0, 2, take_sums, 0)
+
+        @pl.when(is_middle)
+        def _():
+            for k in range(2):
+                pltpu.make_async_copy(sums.at[k], sums.at[k], sent_sums.at[k]).wait()
+                pltpu.make_async_copy(scales.at[k], scales.at[k], sent_scales.at[k]).wait()
 
     def drain(b, _):
         zb, yb = b // ny, b % ny
-        whole(b, sent_core.at[b], base, users)
         straight = yb == y
-
-        @pl.when(jnp.logical_and(straight, jnp.logical_and(zb >= z, not_first)))
+        here = jnp.logical_and(zb - z <= reach, z - zb <= reach)
+
+        @pl.when(here)
+        def _():
+            whole(b, sent_core.at[b], base, users)
+
+        falls = jnp.logical_and(zb >= z, zb - z + 1 <= reach)
+        rises = jnp.logical_and(zb <= z, z - zb + 1 <= reach)
+
+        @pl.when(jnp.logical_and(straight, jnp.logical_and(falls, not_first)))
         def _():
             whole(b, sent_down.at[b], base, users)
 
-        @pl.when(jnp.logical_and(straight, jnp.logical_and(zb <= z, not_last)))
+        @pl.when(jnp.logical_and(straight, jnp.logical_and(rises, not_last)))
         def _():
             whole(b, sent_up.at[b], base, users)
 
-        if ny > 1:
+        if far:
+            layer = jnp.logical_and(jnp.logical_not(straight), zb == z)
+
+            @pl.when(jnp.logical_and(layer, z == 2))
+            def _():
+                whole(b, sent_down.at[b], base, users)
+
+            @pl.when(jnp.logical_and(layer, z == 1))
+            def _():
+                whole(b, sent_up.at[b], base, users)
+
+            inner = jnp.logical_and(is_middle, zb == nz - 1 - z)
+
+            @pl.when(jnp.logical_and(jnp.logical_and(straight, here), jnp.logical_not(inner)))
+            def _():
+                whole(b, sent_side.at[b], base, users)
+
+        elif ny > 1:
             layer = jnp.logical_and(jnp.logical_not(straight), zb == z)
             near = jnp.logical_or(zb == z + 1, zb == z - 1)
 
@@ -229,6 +388,16 @@
     n = nz * ny
     half = block // lax.axis_size("user")
     dma = pltpu.SemaphoreType.DMA
+    tile = min(256, block)
+    remote = [
+        pltpu.VMEM((half, 2 * users), interactions.dtype),
+        pltpu.VMEM((2, block // tile, half, tile), jnp.int16),
+        pltpu.VMEM((2, 8, half), jnp.float32),
+        dma((2,)),
+        dma((2,)),
+        dma((2,)),
+        dma((2,)),
+    ] if has_far(n // ny, ny) else []
     return pl.pallas_call(
         functools.partial(kernel, nz, ny),
         out_shape=pltpu.VMEM((half, n * block), jnp.float32),
@@ -249,9 +418,10 @@
             dma((n,)),
             dma((n,)),
             dma,
+            *remote,
         ],
         compiler_params=pltpu.CompilerParams(
-            collective_id=0, has_side_effects=True, vmem_limit_bytes=40 * 1024 * 1024
+            collective_id=0, has_side_effects=True, vmem_limit_bytes=(44 if remote else 40) * 1024 * 1024
         ),
         cost_estimate=pl.CostEstimate(
             flops=4 * half * users * n * block, bytes_accessed=4 * half * n * block, transcendentals=0

time: 184 us -> 161 us (0.88)
  the two profiles are of different devices: /device:TPU:1 before, /device:TPU:17 now
where the time goes in v3:
time: 161 us
  Pallas kernels  155 us (96%)
  local copies, waits for them, and re-layouts  6.16 us (4%)
    pallas_call x1, Pallas kernels, shards(): pl.pallas_call(functools.partial(kernel, nz, ny), out_shape=pltpu.VMEM((h...  155 us
    unnamed x1, local copies, waits for them, and re-layouts  6.16 us

profile of v3, /device:TPU:17, one launch (start us, length us, event | category | flops | bytes accessed | tf_op | source)
XLA Modules:
  0.0 160.9 jit_solution(17279588804451905747)
XLA Ops:
  0.0 154.7 %shard_map.28 = f32[512,8192]{1,0:T(8,128)S(1)} custom-call(bf16[1024,1024]{1,0:T(8,128)(2,1)} %x_ref.1, s32[8,1,1024]{2,1,0:T(1,128)} %bitcast.1), custom_call_target="tpu_custom_call" | custom-call | flops 17179869184 | bytes 16777216 | tf_op jit(solution)/shard_map/pallas_call | solution.py:401
  154.7 6.2 %copy.4 = f32[512,8192]{1,0:T(8,128)} copy(f32[512,8192]{1,0:T(8,128)S(1)} %shard_map.28) | data formatting | bytes 33554432

commit v4 on v3

--- a/solution.py
+++ b/solution.py
@@ -231,7 +231,15 @@
             def _():
                 take(b0, p)
 
-                if not far:
+                if far:
+                    @pl.when(z == 0)
+                    def _():
+                        to_up(b0, p)
+
+                    @pl.when(z == nz - 1)
+                    def _():
+                        to_down(b0, p)
+                else:
                     @pl.when(p < split)
                     def _():
                         to_down(b0, p)
@@ -253,15 +261,15 @@
 
                         return 0
 
-                    lax.fori_loop(0, PIECES, inward, 0)
+                    lax.fori_loop(0, split, inward, 0)
 
                 @pl.when(jnp.logical_and(s == 2 * PIECES - 1, is_middle))
                 def _():
                     def late(q, _):
-                        to_side(near_end * ny + y, q)
+                        to_side((nz - 1 - z) * ny + y, q)
                         return 0
 
-                    lax.fori_loop(0, PIECES, late, 0)
+                    lax.fori_loop(split, PIECES, late, 0)
 
             lag = 1 if far else 0
             tc, pc = (s + PIECES - lag) // PIECES - 1, (s + PIECES - lag) % PIECES
@@ -281,9 +289,9 @@
             def _():
                 turned(near_end * ny + y, left_far)
 
-            @pl.when(jnp.logical_and(s == 2 * PIECES, is_middle))
-            def _():
-                lax.fori_loop(0, 2, send_sums, 0)
+            @pl.when(jnp.logical_and(jnp.logical_or(s == 2 * PIECES - 1, s == 2 * PIECES), is_middle))
+            def _():
+                send_sums(s - (2 * PIECES - 1), 0)
 
         kinds = 4 if ny > 1 else 2
         tt = t - 1
@@ -344,19 +352,27 @@
         if far:
             layer = jnp.logical_and(jnp.logical_not(straight), zb == z)
 
-            @pl.when(jnp.logical_and(layer, z == 2))
-            def _():
-                whole(b, sent_down.at[b], base, users)
-
-            @pl.when(jnp.logical_and(layer, z == 1))
-            def _():
-                whole(b, sent_up.at[b], base, users)
+            for towards, sems in ((z >= 2, sent_down), (z < 2, sent_up)):
+
+                @pl.when(jnp.logical_and(layer, jnp.logical_and(is_end, towards)))
+                def _():
+                    whole(b, sems.at[b], base, users)
+
+                @pl.when(jnp.logical_and(layer, jnp.logical_and(is_middle, towards)))
+                def _():
+                    whole(b, sems.at[b], base, split * rows)
 
             inner = jnp.logical_and(is_middle, zb == nz - 1 - z)
-
-            @pl.when(jnp.logical_and(jnp.logical_and(straight, here), jnp.logical_not(inner)))
+            outer = jnp.logical_and(is_middle, zb == near_end)
+            plain = jnp.logical_not(jnp.logical_or(inner, outer))
+
+            @pl.when(jnp.logical_and(jnp.logical_and(straight, here), plain))
             def _():
                 whole(b, sent_side.at[b], base, users)
+
+            @pl.when(jnp.logical_and(straight, inner))
+            def _():
+                whole(b, sent_side.at[b], base, (PIECES - split) * rows)
 
         elif ny > 1:
             layer = jnp.logical_and(jnp.logical_not(straight), zb == z)

time: 161 us -> 155 us (0.963)
  the two profiles are of different devices: /device:TPU:17 before, /device:TPU:1 now
where the time goes in v4:
time: 155 us
  Pallas kernels  149 us (96%)
  local copies, waits for them, and re-layouts  6.16 us (4%)
    pallas_call x1, Pallas kernels, shards(): pl.pallas_call(functools.partial(kernel, nz, ny), out_shape=pltpu.VMEM((h...  149 us
    unnamed x1, local copies, waits for them, and re-layouts  6.16 us

profile of v4, /device:TPU:1, one launch (start us, length us, event | category | flops | bytes accessed | tf_op | source)
XLA Modules:
  0.0 155.3 jit_solution(14676352415594943622)
XLA Ops:
  0.0 149.1 %shard_map.28 = f32[512,8192]{1,0:T(8,128)S(1)} custom-call(bf16[1024,1024]{1,0:T(8,128)(2,1)} %x_ref.1, s32[8,1,1024]{2,1,0:T(1,128)} %bitcast.1), custom_call_target="tpu_custom_call" | custom-call | flops 17179869184 | bytes 16777216 | tf_op jit(solution)/shard_map/pallas_call | solution.py:417
  149.1 6.2 %copy.4 = f32[512,8192]{1,0:T(8,128)} copy(f32[512,8192]{1,0:T(8,128)S(1)} %shard_map.28) | data formatting | bytes 33554432

commit v5 on v4

--- a/solution.py
+++ b/solution.py
@@ -8,7 +8,7 @@
 from jax.sharding import PartitionSpec as P
 
 MESH = pl.DeviceIdType.MESH
-PIECES = 8
+PIECES = 4
 LEVELS = 32767
 
 
@@ -20,7 +20,7 @@
            got, got_core, sent_down, sent_up, sent_side, sent_core, loaded, *remote):
     users, block = x_ref.shape
     half = out_ref.shape[0]
-    rows = users // PIECES
+    tile = block // PIECES
     split = PIECES // 2
     group = lax.axis_index("groups")
     me = lax.axis_index("item")
@@ -56,13 +56,17 @@
     def _():
         pl.semaphore_signal(barrier, inc=1, device_id=up, device_id_type=MESH)
 
-    load = pltpu.make_async_copy(x_ref, panel.at[me, pl.ds(base, users)], loaded)
-    load.start()
+    loads = [
+        pltpu.make_async_copy(x_ref.at[:, pl.ds(p * tile, tile)], panel.at[me, p, pl.ds(base, users)], loaded.at[p])
+        for p in range(PIECES)
+    ]
+    for load in loads:
+        load.start()
     wanted = ny + jnp.where(not_first, 1, 0) + jnp.where(not_last, 1, 0)
     pl.semaphore_wait(barrier, wanted)
 
     def place(b, p):
-        return panel.at[b, pl.ds(pl.multiple_of(base + p * rows, rows), rows)]
+        return panel.at[b, p, pl.ds(base, users)]
 
     def send(b, p, sems, recv, device, source=None):
         pltpu.make_async_remote_copy(
@@ -91,55 +95,60 @@
         send(b, p, sent_side, got.at[b, p], side, source)
 
     def to_core(b, p, source=None):
-        send(b, p, sent_core, got_core.at[b], other, source)
+        send(b, p, sent_core, got_core.at[b, p], other, source)
 
     for p in range(PIECES):
-        mine = x_ref.at[pl.ds(p * rows, rows)]
+        mine = x_ref.at[:, pl.ds(p * tile, tile)]
         to_down(me, p, mine)
         to_up(me, p, mine)
         if ny > 1:
             to_side(me, p, mine)
         to_core(me, p, mine)
 
-    def whole(b, sem, start, count):
-        piece = panel.at[b, pl.ds(start, count)]
-        pltpu.make_async_copy(piece, piece, sem).wait()
-
-    def take_core(b):
-        whole(b, got_core.at[b], (1 - core) * users, users)
-
-    tile = min(256, block)
-
-    def product(b):
-        def columns(c, _):
-            cols = pl.ds(pl.multiple_of(c * tile, tile), tile)
-            co = jnp.dot(left[...], panel[b, :, cols], preferred_element_type=jnp.float32)
-            spot = pl.ds(pl.multiple_of(b * block + c * tile, tile), tile)
-            out_ref[:, spot] = co * row_damp[:, :1] * col_damp[b, :, cols]
-            return 0
-
-        lax.fori_loop(0, block // tile, columns, 0)
+    def whole(b, sem, count):
+        pieces = panel.at[b, pl.ds(0, count), pl.ds(base, users)]
+        pltpu.make_async_copy(pieces, pieces, sem).wait()
+
+    def take_core(b, p):
+        piece = panel.at[b, p, pl.ds((1 - core) * users, users)]
+        pltpu.make_async_copy(piece, piece, got_core.at[b, p]).wait()
+
+    def product(b, p):
+        cols = pl.ds(pl.multiple_of(p * tile, tile), tile)
+        spot = pl.ds(pl.multiple_of(b * block + p * tile, tile), tile)
+        co = jnp.dot(left[...], panel[b, p], preferred_element_type=jnp.float32)
+        out_ref[:, spot] = co * row_damp[:, :1] * col_damp[b, :, cols]
+
+    def own_product(p, _):
+        product(me, p)
+        return 0
 
     logs = jnp.log(counts_ref[...].astype(jnp.float32))
     col_damp[...] = jnp.exp(-0.6 * logs)
     mine = counts_ref[me, :, pl.ds(pl.multiple_of(core * half, half), half)].astype(jnp.float32)
     row_damp[...] = jnp.broadcast_to(jnp.exp(-0.4 * jnp.log(mine)), (128, half)).T
-    load.wait()
-    take_core(me)
+    for p in range(PIECES):
+        loads[p].wait()
+        take_core(me, p)
+    if far:
+        @pl.when(is_middle)
+        def _():
+            scales[...] = jnp.zeros_like(scales)
+
     quarter = min(256, users)
 
     def turned(b, target):
         def turn(c, _):
             part = pl.ds(pl.multiple_of(c * quarter, quarter), quarter)
-            own = panel[b, part, pl.ds(pl.multiple_of(core * half, half), half)]
-            target[:, part] = own.astype(jnp.float32).T.astype(target.dtype)
+            for j in range(half // tile):
+                own = panel[b, core * (half // tile) + j, part]
+                target[j * tile:(j + 1) * tile, part] = own.astype(jnp.float32).T.astype(target.dtype)
             return 0
 
         lax.fori_loop(0, 2 * users // quarter, turn, 0)
 
     turned(me, left)
-    product(me)
-    tiles = block // tile
+    lax.fori_loop(0, PIECES, own_product, 0)
 
     def far_block(k):
         return far_end * ny + y + k * (ny - 1 - 2 * y)
@@ -154,25 +163,18 @@
             src_ref=scales.at[k], dst_ref=scales.at[k], send_sem=sent_scales.at[k], recv_sem=got_scales.at[k],
             device_id=at(near_end, y), device_id_type=MESH)
 
-    def send_sums(k, _):
-        b = far_block(k)
-        take_core(b)
-        scales[k] = jnp.zeros((8, half), jnp.float32)
-
-        def columns(c, _):
-            cols = pl.ds(pl.multiple_of(c * tile, tile), tile)
-            co = jnp.dot(left_far[...], panel[b, :, cols], preferred_element_type=jnp.float32)
-            most = jnp.maximum(jnp.max(co, axis=1, keepdims=True), 1e-30)
-            level = (co * (2 * LEVELS / most) + 0.5).astype(jnp.int32) - LEVELS
-            sums[k, c] = level.astype(jnp.int16)
-            unit = jnp.broadcast_to(most * (0.5 / LEVELS), (half, 128)).T
-            scales[k, pl.ds(c, 1), :] = unit[0:1]
-            sums_copy(k, c).start()
-            return 0
-
-        lax.fori_loop(0, tiles, columns, 0)
-        scales_copy(k).start()
-        return 0
+    def send_sums(k, c):
+        co = jnp.dot(left_far[...], panel[far_block(k), c], preferred_element_type=jnp.float32)
+        most = jnp.maximum(jnp.max(co, axis=1, keepdims=True), 1e-30)
+        level = (co * (2 * LEVELS / most) + 0.5).astype(jnp.int32) - LEVELS
+        sums[k, c] = level.astype(jnp.int16)
+        unit = jnp.broadcast_to(most * (0.5 / LEVELS), (half, 128)).T
+        scales[k, pl.ds(c, 1), :] = unit[0:1]
+        sums_copy(k, c).start()
+
+        @pl.when(c == PIECES - 1)
+        def _():
+            scales_copy(k).start()
 
     def take_sums(k, _):
         b = far_end_of_end() * ny + y + k * (ny - 1 - 2 * y)
@@ -188,7 +190,7 @@
             out_ref[:, spot] = co * row_damp[:, :1] * col_damp[b, :, cols]
             return 0
 
-        lax.fori_loop(0, tiles, columns, 0)
+        lax.fori_loop(0, PIECES, columns, 0)
         return 0
 
     def far_end_of_end():
@@ -221,6 +223,19 @@
                     def _():
                         to_side(b, p)
                 to_core(b, p)
+
+        def multiply(b, q, k, summed):
+            take_core(b, q)
+            if far:
+                @pl.when(jnp.logical_and(is_middle, summed))
+                def _():
+                    send_sums(k, q)
+            product(b, q)
+
+        def along_product(zb):
+            @pl.when(jnp.logical_and(t < reach, jnp.logical_and(zb >= 0, zb < nz)))
+            def _():
+                multiply(zb * ny + y, p, 0, t == 1)
 
         along(z + 1 + t, to_down)
         along(z - 1 - t, to_up)
@@ -285,39 +300,28 @@
             crossed(z - distance(tc))
 
         if far:
-            @pl.when(jnp.logical_and(s == 2 * PIECES - 2, is_middle))
+            @pl.when(jnp.logical_and(s == PIECES, is_middle))
             def _():
                 turned(near_end * ny + y, left_far)
 
-            @pl.when(jnp.logical_and(jnp.logical_or(s == 2 * PIECES - 1, s == 2 * PIECES), is_middle))
-            def _():
-                send_sums(s - (2 * PIECES - 1), 0)
-
-        kinds = 4 if ny > 1 else 2
-        tt = t - 1
-        kind = p // (PIECES // 4)
-        back, crossing = kind % 2, kind // 2
-        gap = jnp.where(crossing == 1, jnp.where(tt == 0, 0, distance(tt)), tt + 1)
-        zb = z + (1 - 2 * back) * gap
-        yb = y + crossing * (ny - 1 - 2 * y)
-        fits = jnp.logical_and(jnp.logical_and(zb >= 0, zb < nz), jnp.logical_and(gap <= reach, tt <= reach))
-        turn_now = jnp.logical_and(p % (PIECES // 4) == 0, kind < kinds)
-        first = jnp.logical_and(turn_now, jnp.logical_or(tt > 0, jnp.logical_and(tt == 0, kind < 3)))
-
-        @pl.when(jnp.logical_and(fits, first))
-        def _():
-            b = zb * ny + yb
-            if far:
-                @pl.when(jnp.logical_or(is_end, tt != 1))
-                def _():
-                    take_core(b)
-            else:
-                take_core(b)
-            product(b)
+        along_product(z + 1 + t)
+        along_product(z - 1 - t)
+        if ny > 1:
+            @pl.when(t == 0)
+            def _():
+                multiply(b0, p, 1, t > 0)
+
+            def crossed_product(zb):
+                @pl.when(jnp.logical_and(reached(tc), jnp.logical_and(zb >= 0, zb < nz)))
+                def _():
+                    multiply(zb * ny + (ny - 1 - y), pc, 1, tc == 1)
+
+            crossed_product(z + distance(tc))
+            crossed_product(z - distance(tc))
 
         return 0
 
-    lax.fori_loop(0, (reach + 2) * PIECES, step, 0)
+    lax.fori_loop(0, (reach + 1) * PIECES + (1 if far else 0), step, 0)
     if far:
         @pl.when(is_end)
         def _():
@@ -336,18 +340,18 @@
 
         @pl.when(here)
         def _():
-            whole(b, sent_core.at[b], base, users)
+            whole(b, sent_core.at[b], PIECES)
 
         falls = jnp.logical_and(zb >= z, zb - z + 1 <= reach)
         rises = jnp.logical_and(zb <= z, z - zb + 1 <= reach)
 
         @pl.when(jnp.logical_and(straight, jnp.logical_and(falls, not_first)))
         def _():
-            whole(b, sent_down.at[b], base, users)
+            whole(b, sent_down.at[b], PIECES)
 
         @pl.when(jnp.logical_and(straight, jnp.logical_and(rises, not_last)))
         def _():
-            whole(b, sent_up.at[b], base, users)
+            whole(b, sent_up.at[b], PIECES)
 
         if far:
             layer = jnp.logical_and(jnp.logical_not(straight), zb == z)
@@ -356,11 +360,11 @@
 
                 @pl.when(jnp.logical_and(layer, jnp.logical_and(is_end, towards)))
                 def _():
-                    whole(b, sems.at[b], base, users)
+                    whole(b, sems.at[b], PIECES)
 
                 @pl.when(jnp.logical_and(layer, jnp.logical_and(is_middle, towards)))
                 def _():
-                    whole(b, sems.at[b], base, split * rows)
+                    whole(b, sems.at[b], split)
 
             inner = jnp.logical_and(is_middle, zb == nz - 1 - z)
             outer = jnp.logical_and(is_middle, zb == near_end)
@@ -368,11 +372,11 @@
 
             @pl.when(jnp.logical_and(jnp.logical_and(straight, here), plain))
             def _():
-                whole(b, sent_side.at[b], base, users)
+                whole(b, sent_side.at[b], PIECES)
 
             @pl.when(jnp.logical_and(straight, inner))
             def _():
-                whole(b, sent_side.at[b], base, (PIECES - split) * rows)
+                whole(b, sent_side.at[b], PIECES - split)
 
         elif ny > 1:
             layer = jnp.logical_and(jnp.logical_not(straight), zb == z)
@@ -380,19 +384,19 @@
 
             @pl.when(jnp.logical_and(layer, not_first))
             def _():
-                whole(b, sent_down.at[b], base, split * rows)
+                whole(b, sent_down.at[b], split)
 
             @pl.when(jnp.logical_and(layer, not_last))
             def _():
-                whole(b, sent_up.at[b], base, split * rows)
+                whole(b, sent_up.at[b], split)
 
             @pl.when(jnp.logical_and(straight, near))
             def _():
-                whole(b, sent_side.at[b], base, (PIECES - split) * rows)
+                whole(b, sent_side.at[b], PIECES - split)
 
             @pl.when(jnp.logical_and(straight, jnp.logical_not(near)))
             def _():
-                whole(b, sent_side.at[b], base, users)
+                whole(b, sent_side.at[b], PIECES)
 
         return 0
 
@@ -404,7 +408,7 @@
     n = nz * ny
     half = block // lax.axis_size("user")
     dma = pltpu.SemaphoreType.DMA
-    tile = min(256, block)
+    tile = block // PIECES
     remote = [
         pltpu.VMEM((half, 2 * users), interactions.dtype),
         pltpu.VMEM((2, block // tile, half, tile), jnp.int16),
@@ -423,17 +427,17 @@
         ],
         out_specs=pl.BlockSpec(memory_space=pltpu.VMEM),
         scratch_shapes=[
-            pltpu.VMEM((n, 2 * users, block), interactions.dtype),
+            pltpu.VMEM((n, PIECES, 2 * users, block // PIECES), interactions.dtype),
             pltpu.VMEM((half, 2 * users), interactions.dtype),
             pltpu.VMEM((half, 128), jnp.float32),
             pltpu.VMEM((n, 1, block), jnp.float32),
+            dma((n, PIECES)),
             dma((n, PIECES)),
             dma((n,)),
             dma((n,)),
             dma((n,)),
             dma((n,)),
-            dma((n,)),
-            dma,
+            dma((PIECES,)),
             *remote,
         ],
         compiler_params=pltpu.CompilerParams(

time: 155 us -> 153 us (0.987)
  Pallas kernels: 149 us -> 147 us
    pallas_call x1, Pallas kernels: 149 us -> 147 us  [shards(): pl.pallas_call(functools.partial(kernel, nz, ny), out_shape=pltpu.VMEM((h...]
where the time goes in v5:
time: 153 us
  Pallas kernels  147 us (96%)
  local copies, waits for them, and re-layouts  6.16 us (4%)
    pallas_call x1, Pallas kernels, shards(): pl.pallas_call(functools.partial(kernel, nz, ny), out_shape=pltpu.VMEM((h...  147 us
    unnamed x1, local copies, waits for them, and re-layouts  6.16 us

profile of v5, /device:TPU:1, one launch (start us, length us, event | category | flops | bytes accessed | tf_op | source)
XLA Modules:
  0.0 152.8 jit_solution(9972050163503240877)
XLA Ops:
  0.0 146.7 %shard_map.28 = f32[512,8192]{1,0:T(8,128)S(1)} custom-call(bf16[1024,1024]{1,0:T(8,128)(2,1)} %x_ref.1, s32[8,1,1024]{2,1,0:T(1,128)} %bitcast.1), custom_call_target="tpu_custom_call" | custom-call | flops 17179869184 | bytes 16777216 | tf_op jit(solution)/shard_map/pallas_call | solution.py:421
  146.7 6.2 %copy.4 = f32[512,8192]{1,0:T(8,128)} copy(f32[512,8192]{1,0:T(8,128)S(1)} %shard_map.28) | data formatting | bytes 33554432

commit v6 on v5

--- a/solution.py
+++ b/solution.py
@@ -130,11 +130,6 @@
     for p in range(PIECES):
         loads[p].wait()
         take_core(me, p)
-    if far:
-        @pl.when(is_middle)
-        def _():
-            scales[...] = jnp.zeros_like(scales)
-
     quarter = min(256, users)
 
     def turned(b, target):
@@ -155,13 +150,13 @@
 
     def sums_copy(k, c):
         return pltpu.make_async_remote_copy(
-            src_ref=sums.at[k, c], dst_ref=sums.at[k, c], send_sem=sent_sums.at[k], recv_sem=got_sums.at[k],
+            src_ref=sums.at[k, c], dst_ref=sums.at[k, c], send_sem=sent_sums.at[k], recv_sem=got_sums.at[k, c],
             device_id=at(near_end, y), device_id_type=MESH)
 
-    def scales_copy(k):
+    def scales_copy(k, c):
         return pltpu.make_async_remote_copy(
-            src_ref=scales.at[k], dst_ref=scales.at[k], send_sem=sent_scales.at[k], recv_sem=got_scales.at[k],
-            device_id=at(near_end, y), device_id_type=MESH)
+            src_ref=scales.at[k, c], dst_ref=scales.at[k, c], send_sem=sent_scales.at[k],
+            recv_sem=got_scales.at[k, c], device_id=at(near_end, y), device_id_type=MESH)
 
     def send_sums(k, c):
         co = jnp.dot(left_far[...], panel[far_block(k), c], preferred_element_type=jnp.float32)
@@ -169,29 +164,20 @@
         level = (co * (2 * LEVELS / most) + 0.5).astype(jnp.int32) - LEVELS
         sums[k, c] = level.astype(jnp.int16)
         unit = jnp.broadcast_to(most * (0.5 / LEVELS), (half, 128)).T
-        scales[k, pl.ds(c, 1), :] = unit[0:1]
+        scales[k, c] = unit[0:1]
+        scales_copy(k, c).start()
         sums_copy(k, c).start()
 
-        @pl.when(c == PIECES - 1)
-        def _():
-            scales_copy(k).start()
-
-    def take_sums(k, _):
+    def take_sums(k, c):
         b = far_end_of_end() * ny + y + k * (ny - 1 - 2 * y)
-        pltpu.make_async_copy(sums.at[k], sums.at[k], got_sums.at[k]).wait()
-        pltpu.make_async_copy(scales.at[k], scales.at[k], got_scales.at[k]).wait()
-
-        def columns(c, _):
-            cols = pl.ds(pl.multiple_of(c * tile, tile), tile)
-            unit = jnp.broadcast_to(scales[k, pl.ds(c, 1), :], (128, half)).T
-            level = sums[k, c].astype(jnp.int32) + LEVELS
-            co = level.astype(jnp.float32) * unit[:, :1]
-            spot = pl.ds(pl.multiple_of(b * block + c * tile, tile), tile)
-            out_ref[:, spot] = co * row_damp[:, :1] * col_damp[b, :, cols]
-            return 0
-
-        lax.fori_loop(0, PIECES, columns, 0)
-        return 0
+        pltpu.make_async_copy(scales.at[k, c], scales.at[k, c], got_scales.at[k, c]).wait()
+        pltpu.make_async_copy(sums.at[k, c], sums.at[k, c], got_sums.at[k, c]).wait()
+        cols = pl.ds(pl.multiple_of(c * tile, tile), tile)
+        unit = jnp.broadcast_to(scales[k, c], (128, half)).T
+        level = sums[k, c].astype(jnp.int32) + LEVELS
+        co = level.astype(jnp.float32) * unit[:, :1]
+        spot = pl.ds(pl.multiple_of(b * block + c * tile, tile), tile)
+        out_ref[:, spot] = co * row_damp[:, :1] * col_damp[b, :, cols]
 
     def far_end_of_end():
         return nz - 1 - z
@@ -319,14 +305,16 @@
             crossed_product(z + distance(tc))
             crossed_product(z - distance(tc))
 
+        if far:
+            @pl.when(jnp.logical_and(is_end, tc == 2))
+            def _():
+                take_sums(0, pc)
+                take_sums(1, pc)
+
         return 0
 
     lax.fori_loop(0, (reach + 1) * PIECES + (1 if far else 0), step, 0)
     if far:
-        @pl.when(is_end)
-        def _():
-            lax.fori_loop(0, 2, take_sums, 0)
-
         @pl.when(is_middle)
         def _():
             for k in range(2):
@@ -412,11 +400,11 @@
     remote = [
         pltpu.VMEM((half, 2 * users), interactions.dtype),
         pltpu.VMEM((2, block // tile, half, tile), jnp.int16),
-        pltpu.VMEM((2, 8, half), jnp.float32),
+        pltpu.VMEM((2, PIECES, 1, half), jnp.float32),
         dma((2,)),
+        dma((2, PIECES)),
         dma((2,)),
-        dma((2,)),
-        dma((2,)),
+        dma((2, PIECES)),
     ] if has_far(n // ny, ny) else []
     return pl.pallas_call(
         functools.partial(kernel, nz, ny),

time: 153 us -> 151 us (0.987)
  Pallas kernels: 147 us -> 145 us
    pallas_call x1, Pallas kernels: 147 us -> 145 us  [shards(): pl.pallas_call(functools.partial(kernel, nz, ny), out_shape=pltpu.VMEM((h...]
where the time goes in v6:
time: 151 us
  Pallas kernels  145 us (96%)
  local copies, waits for them, and re-layouts  6.16 us (4%)
    pallas_call x1, Pallas kernels, shards(): pl.pallas_call(functools.partial(kernel, nz, ny), out_shape=pltpu.VMEM((h...  145 us
    unnamed x1, local copies, waits for them, and re-layouts  6.16 us

profile of v6, /device:TPU:1, one launch (start us, length us, event | category | flops | bytes accessed | tf_op | source)
XLA Modules:
  0.0 151.2 jit_solution(12529188581294993928)
XLA Ops:
  0.0 145.0 %shard_map.28 = f32[512,8192]{1,0:T(8,128)S(1)} custom-call(bf16[1024,1024]{1,0:T(8,128)(2,1)} %x_ref.1, s32[8,1,1024]{2,1,0:T(1,128)} %bitcast.1), custom_call_target="tpu_custom_call" | custom-call | flops 17179869184 | bytes 16777216 | tf_op jit(solution)/shard_map/pallas_call | solution.py:409
  145.0 6.2 %copy.4 = f32[512,8192]{1,0:T(8,128)} copy(f32[512,8192]{1,0:T(8,128)S(1)} %shard_map.28) | data formatting | bytes 33554432
